TPU v7x, 32 devices: a whole 2x2x4 slice. The times are simulated.
32 devices in a mesh: ctx: 8 (over z, y), grp: 4 (over x, core).
Axes of the slice: x: 2, y: 2, z: 4, core: 2. Of those that a mesh axis runs over, the one named last changes fastest.
Arguments:
- queries: bfloat16 [4, 4096, 512], P('grp', 'ctx'), as said below
- keys: bfloat16 [4, 4096, 512], P('grp', 'ctx'), as said below
- values: bfloat16 [4, 4096, 512], P('grp', 'ctx'), may hold values from -6 to 6
- summary_pos: int32 [4, 8, 8], P('grp', 'ctx'), may hold values from 0 to 511, as said below
Outputs:
- attended: bfloat16 [4, 4096, 512], P('grp', 'ctx')
Inputs may be any that keep to these rules, and one draw needn't show every extreme that they name: queries' entries lie within -320 and 320. keys' entries lie within -6 and 6. `summary_pos`: in each block the j-th summary position lies in [j * 64, (j + 1) * 64); the last one is 511.
All inputs are finite; a program needn't handle non-finite values.
Results may differ from a plain program's by a relative error of at most 0.0045.
Values may be sent and summed in bfloat16 or wider, within the bound.
A program may use at most 64 MiB of HBM per device.

v0:
```python
import math

import jax
import jax.numpy as jnp
from jax import lax
from jax.sharding import PartitionSpec as P

H = 8
HD = 64
BLK = 512
SUMM = 8


masked_score = -1e30


def shifted(value, axis, steps):
    count = lax.axis_size(axis)
    pairs = [(source, (source + steps) % count) for source in range(count)]
    return lax.ppermute(value, axis, pairs)


def shifted_2(value, axis, by):
    count = lax.axis_size(axis)
    pairs = [(i, i + by) for i in range(count) if 0 <= i + by < count]
    return lax.ppermute(value, axis, pairs)


def fold_rows(running, qheads, qblock, summary_rows, row_block, score_scale):
    half_width = summary_rows.shape[1] // 2
    head_count = running[0].shape[0]
    head_size = half_width // head_count

    def update(current, tile_pair):
        piece_rows, blocks = tile_pair
        peak_old, total_old, summed_old = current
        tile_keys = piece_rows[:, :half_width].reshape(-1, head_count, head_size)
        tile_vals = piece_rows[:, half_width:].reshape(-1, head_count, head_size)
        scores = (
            jnp.einsum("qhd,rhd->hqr", qheads, tile_keys, preferred_element_type=jnp.float32)
            * score_scale
        )
        allowed = (blocks[None, :] <= qblock[:, None] - 2)[None]
        scores = jnp.where(allowed, scores, masked_score)
        higher = jnp.maximum(peak_old, scores.max(-1))
        weights = jnp.where(allowed, jnp.exp(scores - higher[..., None]), 0.0)
        rescale = jnp.exp(peak_old - higher)
        total_new = total_old * rescale + weights.sum(-1)
        summed_new = summed_old * rescale[..., None] + jnp.einsum(
            "hqr,rhd->hqd",
            weights.astype(jnp.bfloat16),
            tile_vals,
            preferred_element_type=jnp.float32,
        )
        return ((higher, total_new, summed_new), None)

    row_count = summary_rows.shape[0]
    if row_count > 512 and row_count % 512 == 0:
        tile_list = (
            summary_rows.reshape(row_count // 512, 512, -1),
            row_block.reshape(row_count // 512, 512),
        )
        result, unused = lax.scan(update, running, tile_list)
        return result
    result, unused = update(running, (summary_rows, row_block))
    return result


def shards(queries, keys, values, summary_pos):
    ctx_count = lax.axis_size("ctx")
    ctx_index = lax.axis_index("ctx")
    grp_index = lax.axis_index("grp")
    device_flat = grp_index * ctx_count + ctx_index
    tokens_here = queries.shape[1]
    model_width = queries.shape[2]
    blocks_here = tokens_here // BLK
    score_scale = 1.0 / math.sqrt(HD)
    qheads = queries[0].reshape(tokens_here, H, HD)
    paired = jnp.concatenate([keys[0], values[0]], axis=-1)
    from_ctx = shifted(paired, "ctx", 1)
    from_grp = shifted_2(from_ctx, "grp", 1)
    previous = jnp.where(ctx_index == 0, from_grp, from_ctx)
    own_blocks = paired.reshape(blocks_here, BLK, 2 * model_width)
    prev_blocks = jnp.concatenate([previous[None], own_blocks[:-1]], axis=0)
    window = jnp.concatenate([prev_blocks, own_blocks], axis=1)
    near_keys = window[..., :model_width].reshape(blocks_here, 2 * BLK, H, HD)
    near_vals = window[..., model_width:].reshape(blocks_here, 2 * BLK, H, HD)
    block_ids = device_flat * blocks_here + jnp.arange(blocks_here, dtype=jnp.int32)
    near_scores = (
        jnp.einsum(
            "bqhd,bkhd->bhqk",
            qheads.reshape(blocks_here, BLK, H, HD),
            near_keys,
            preferred_element_type=jnp.float32,
        )
        * score_scale
    )
    window_index = jnp.arange(2 * BLK, dtype=jnp.int32)
    query_index = jnp.arange(BLK, dtype=jnp.int32)
    own_part = (window_index[None, :] >= BLK) & (
        window_index[None, :] - BLK <= query_index[:, None]
    )
    prev_part = (window_index[None, None, :] < BLK) & (block_ids >= 1)[:, None, None]
    near_mask = (own_part[None] | prev_part)[:, None]
    near_scores = jnp.where(near_mask, near_scores, masked_score)
    near_peak = near_scores.max(-1)
    near_weight = jnp.where(near_mask, jnp.exp(near_scores - near_peak[..., None]), 0.0)
    near_total = near_weight.sum(-1)
    near_summed = jnp.einsum(
        "bhqk,bkhd->bhqd",
        near_weight.astype(jnp.bfloat16),
        near_vals,
        preferred_element_type=jnp.float32,
    )
    running = (
        jnp.transpose(near_peak, (1, 0, 2)).reshape(H, tokens_here),
        jnp.transpose(near_total, (1, 0, 2)).reshape(H, tokens_here),
        jnp.transpose(near_summed, (1, 0, 2, 3)).reshape(H, tokens_here, HD),
    )
    qblock = device_flat * blocks_here + jnp.arange(tokens_here, dtype=jnp.int32) // BLK
    offsets = (jnp.arange(blocks_here, dtype=jnp.int32)[:, None] * BLK + summary_pos[0]).reshape(-1)
    local_summ = paired[offsets]
    summ_here = local_summ.shape[0]
    slot_block = jnp.arange(summ_here, dtype=jnp.int32) // SUMM
    per_group = lax.all_gather(local_summ[None, None], "ctx", axis=1, tiled=True)
    shard_piece = lax.all_gather(per_group, "grp", axis=0, tiled=True)
    group_ids = jnp.arange(shard_piece.shape[0], dtype=jnp.int32)
    row_blocks = (
        (
            group_ids[:, None, None] * ctx_count
            + jnp.arange(ctx_count, dtype=jnp.int32)[None, :, None]
        )
        * blocks_here
        + slot_block[None, None, :]
    ).reshape(-1)
    running = fold_rows(
        running, qheads, qblock, shard_piece.reshape(-1, 2 * model_width), row_blocks, score_scale
    )
    result = running[2] / running[1][..., None]
    return (
        jnp.transpose(result, (1, 0, 2))
        .reshape(tokens_here, model_width)
        .astype(jnp.bfloat16)[None]
    )


def solution(mesh):
    placed = (
        P("grp", "ctx", None),
        P("grp", "ctx", None),
        P("grp", "ctx", None),
        P("grp", "ctx", None),
    )
    return jax.shard_map(
        shards, mesh=mesh, in_specs=placed, out_specs=P("grp", "ctx", None), check_vma=False
    )
```

profile of v0, /device:TPU:1, one launch (start us, length us, event | category | flops | bytes accessed | tf_op | source)
XLA Modules:
  0.0 103.8 jit_solution(17755802643930758737)
XLA Ops:
  0.0 1.5 %fusion.43 = (bf16[1,512,1024]{2,1,0:T(8,128)(2,1)S(1)}, bf16[512,1024]{1,0:T(8,128)(2,1)S(1)}) fusion(bf16[512,512]{1,0:T(8,128)(2,1)} %bitcast.86, bf16[512,512]{1,0:T(8,128)(2,1)} %bitcast.87), kind=kLoop, calls=%fused_computation.63 | loop fusion | flops 2097152 | bytes 3145728 | tf_op jit(solution)/shard_map/reshape | solution.py:83
  1.5 2.1 %collective-permute-start = (bf16[512,1024]{1,0:T(8,128)(2,1)S(1)}, bf16[512,1024]{1,0:T(8,128)(2,1)}, u32[]{:S(2)}, u32[]{:S(2)}) collective-permute-start(bf16[512,1024]{1,0:T(8,128)(2,1)S(1)} %get-tuple-element.10), channel_id=1, source_target_pairs={{0,4},{4,8},{8,12},{12,16},{16,20},{20,24},{24,28},{28,0},{1,5},{5... | collective-permute-start | bytes 3145736 | tf_op jit(solution)/shard_map/ppermute | solution.py:20
  3.6 0.7 fusion.36
  4.3 0.6 gather_fusion
  4.9 43.3 %all-gather = bf16[64,1024]{1,0:T(8,128)(2,1)S(1)} all-gather(bf16[8,1024]{1,0:T(8,128)(2,1)S(1)} %gather_fusion), channel_id=2, replica_groups=mesh['ctx'=8,'grp'=4] {'ctx'}, dimensions={0}, use_global_device_ids=true | all-gather | bytes 147456 | tf_op jit(solution)/shard_map/all_gather | solution.py:125
  48.2 13.6 %all_gather.7 = bf16[4,8,8,1024]{3,2,1,0:T(8,128)(2,1)S(1)} all-gather(bf16[1,8,8,1024]{3,2,1,0:T(8,128)(2,1)S(1)} %bitcast.84), channel_id=1, replica_groups=mesh['ctx'=8,'grp'=4] {'grp'}, dimensions={0}, use_global_device_ids=true | all-gather | bytes 655360 | tf_op jit(solution)/shard_map/all_gather | solution.py:126
  61.7 0.1 iota_add_fusion.1
  61.8 0.1 broadcast_add_fusion
  61.9 0.0 collective-permute-done
  61.9 2.5 %collective-permute-start.1 = (bf16[512,1024]{1,0:T(8,128)(2,1)}, bf16[512,1024]{1,0:T(8,128)(2,1)}, u32[]{:S(2)}, u32[]{:S(2)}) collective-permute-start(bf16[512,1024]{1,0:T(8,128)(2,1)} %collective-permute-done), channel_id=1, source_target_pairs={{0,1},{1,2},{2,3},{4,5},{5,6},{6,7},{8,9},{9,10},{10,11},{12,13},{... | collective-permute-start | bytes 3145736 | tf_op jit(solution)/shard_map/ppermute | solution.py:26
  64.5 0.0 copy-done.2
  64.5 0.2 copy.22
  64.7 0.1 add.103
  64.8 0.1 copy.25
  64.9 0.1 copy.26
  65.1 0.1 broadcast_compare_fusion
  65.2 0.9 fusion.12
  66.2 3.4 %fusion.6 = (f32[8,512]{1,0:T(8,128)}, f32[8,256,512]{2,1,0:T(8,128)}) fusion(pred[512,256]{0,1:T(8,128)(4,1)S(1)} %broadcast_compare_fusion, bf16[256,8,64]{0,2,1:T(8,128)(2,1)S(1)} %bitcast.82, bf16[512,8,64]{0,2,1:T(8,128)(2,1)S(1)} %bitcast.78), kind=kOutput, calls=%fused_computation.10 | convolution fusion | flops 137359360 | bytes 5128192 | tf_op jit(solution)/shard_map/qhd,rhd->hqr/dot_general | solution.py:40
  69.6 6.9 %collective-permute-done.1 = bf16[512,1024]{1,0:T(8,128)(2,1)} collective-permute-done((bf16[512,1024]{1,0:T(8,128)(2,1)}, bf16[512,1024]{1,0:T(8,128)(2,1)}, u32[]{:S(2)}, u32[]{:S(2)}) %collective-permute-start.1) | collective-permute-done | bytes 1048608 | tf_op jit(solution)/shard_map/ppermute | solution.py:26
  76.5 1.3 %select_bitcast_fusion = bf16[1,512,1024]{2,1,0:T(8,128)(2,1)S(1)} fusion(bf16[512,1024]{1,0:T(8,128)(2,1)} %collective-permute-done.1, bf16[512,1024]{1,0:T(8,128)(2,1)} %collective-permute-done, pred[]{:T(512)S(6)} %eq.3), kind=kLoop, calls=%fused_computation.28 | loop fusion | flops 524288 | bytes 3145729 | tf_op jit(solution)/shard_map/broadcast_in_dim | solution.py:84
  77.8 1.1 %fusion.26 = (bf16[1,1024,512]{2,1,0:T(8,128)(2,1)S(1)}, bf16[1,1024,512]{2,1,0:T(8,128)(2,1)}) fusion(bf16[1,512,1024]{2,1,0:T(8,128)(2,1)S(1)} %select_bitcast_fusion, bf16[1,512,1024]{2,1,0:T(8,128)(2,1)S(1)} %get-tuple-element.9), kind=kLoop, calls=%fused_computation.24 | loop fusion | flops 4194304 | bytes 4194304 | tf_op jit(solution)/shard_map/concatenate | solution.py:85
  79.0 1.5 %copy.21 = bf16[1,1024,512]{1,2,0:T(8,128)(2,1)S(1)} copy(bf16[1,1024,512]{2,1,0:T(8,128)(2,1)} %get-tuple-element.8) | data formatting | bytes 2097152 | tf_op jit(solution)/shard_map/slice | solution.py:86
  80.5 2.8 %fusion = (f32[8,512]{1,0:T(8,128)S(1)}, f32[8,1024,512]{2,1,0:T(8,128)S(1)}) fusion(pred[512,1024]{0,1:T(8,128)(4,1)S(1)} %fusion.12, bf16[1024,8,64]{0,2,1:T(8,128)(2,1)S(1)} %bitcast.80, bf16[512,8,64]{0,2,1:T(8,128)(2,1)S(1)} %bitcast.79), kind=kOutput, calls=%fused_computation.3 | convolution fusion | flops 549449728 | bytes 18890752 | tf_op jit(solution)/shard_map/bqhd,bkhd->bhqk/dot_general | solution.py:90
  83.3 0.0 copy-start.3
  83.3 4.0 %fusion.1 = f32[8,512]{1,0:T(8,128)S(1)} fusion(f32[8,1024,512]{2,1,0:T(8,128)S(1)} %get-tuple-element.14, f32[8,512]{1,0:T(8,128)S(1)} %get-tuple-element.13, pred[512,1024]{0,1:T(8,128)(4,1)S(1)} %fusion.12), kind=kLoop, calls=%fused_computation.4 | loop fusion | flops 20967424 | bytes 17334272 | tf_op jit(solution)/shard_map/reduce_sum | solution.py:108
  87.3 3.0 %copy-done = f32[8,1024,512]{2,1,0:T(8,128)} copy-done((f32[8,1024,512]{2,1,0:T(8,128)}, f32[8,1024,512]{2,1,0:T(8,128)S(1)}, u32[]{:S(2)}) %copy-start) | copy-done | bytes 16777240
  90.3 0.0 copy-done.3
  90.4 1.0 fusion.7
  91.4 2.3 %fusion.17 = f32[512,8,64]{0,2,1:T(8,128)} fusion(bf16[256,8,64]{0,2,1:T(8,128)(2,1)S(1)} %bitcast.88, f32[8,256,512]{2,1,0:T(8,128)S(1)} %copy-done.1, f32[8,512]{1,0:T(8,128)S(1)} %max.18, pred[512,256]{0,1:T(8,128)(4,1)S(1)} %broadcast_compare_fusion), kind=kOutput, calls=%fused_computation.21 | convolution fusion | flops 139460608 | bytes 5652480 | tf_op jit(solution)/shard_map/hqr,rhd->hqd/dot_general | solution.py:49
  93.7 0.5 copy.23
  94.2 8.5 %divide_convert_fusion = bf16[512,8,64]{0,2,1:T(8,128)(2,1)S(1)} fusion(f32[512,8,64]{0,2,1:T(8,128)} %fusion.17, bf16[1024,8,64]{0,2,1:T(8,128)(2,1)S(1)} %bitcast.83, f32[8,1024,512]{2,1,0:T(8,128)} %copy-done, f32[8,512]{1,0:T(8,128)S(1)} %get-tuple-element.13, pred[512,1024]{0,1:T(8,128)(4,1)S(1)} %fusion.12, f32[512,8]{0,1:T(8,128)S(1)} %get-tuple-element.5, ...), kind=kOutput, calls=%fused_computation.27 | convolution fusion | flops 558891008 | bytes 19972096 | tf_op jit(solution)/shard_map/bhqk,bkhd->bhqd/dot_general | solution.py:109
  102.8 1.0 copy.28
  (13 shorter events, 0.1 us)
Async XLA Ops:
  0.0 64.5 %copy-start.2 = (bf16[1,512,512]{2,1,0:T(8,128)(2,1)S(1)}, bf16[1,512,512]{2,1,0:T(8,128)(2,1)}, u32[]{:S(2)}) copy-start(bf16[1,512,512]{2,1,0:T(8,128)(2,1)} %param.4) | copy-start | bytes 1572868
  1.5 60.4 %collective-permute-start = (bf16[512,1024]{1,0:T(8,128)(2,1)S(1)}, bf16[512,1024]{1,0:T(8,128)(2,1)}, u32[]{:S(2)}, u32[]{:S(2)}) collective-permute-start(bf16[512,1024]{1,0:T(8,128)(2,1)S(1)} %get-tuple-element.10), channel_id=1, source_target_pairs={{0,4},{4,8},{8,12},{12,16},{16,20},{20,24},{24,28},{28,0},{1,5},{5... | collective-permute-start | bytes 3145736 | tf_op jit(solution)/shard_map/ppermute | solution.py:20
  61.9 14.6 %collective-permute-start.1 = (bf16[512,1024]{1,0:T(8,128)(2,1)}, bf16[512,1024]{1,0:T(8,128)(2,1)}, u32[]{:S(2)}, u32[]{:S(2)}) collective-permute-start(bf16[512,1024]{1,0:T(8,128)(2,1)} %collective-permute-done), channel_id=1, source_target_pairs={{0,1},{1,2},{2,3},{4,5},{5,6},{6,7},{8,9},{9,10},{10,11},{12,13},{... | collective-permute-start | bytes 3145736 | tf_op jit(solution)/shard_map/ppermute | solution.py:26
  83.2 7.1 %copy-start = (f32[8,1024,512]{2,1,0:T(8,128)}, f32[8,1024,512]{2,1,0:T(8,128)S(1)}, u32[]{:S(2)}) copy-start(f32[8,1024,512]{2,1,0:T(8,128)S(1)} %get-tuple-element.14) | copy-start | bytes 50331652
  83.3 7.1 %copy-start.3 = (f32[8,512]{1,0:T(8,128)S(1)}, f32[8,512]{1,0:T(8,128)}, u32[]{:S(2)}) copy-start(f32[8,512]{1,0:T(8,128)} %get-tuple-element.15) | copy-start | bytes 49156
  83.3 7.1 %copy-start.1 = (f32[8,256,512]{2,1,0:T(8,128)S(1)}, f32[8,256,512]{2,1,0:T(8,128)}, u32[]{:S(2)}) copy-start(f32[8,256,512]{2,1,0:T(8,128)} %get-tuple-element.16) | copy-start | bytes 12582916
where the time goes:
time: 104 us
  blocking collectives  56.9 us (55%)
  matrix products  17 us (16%)
  other arithmetic  11 us (11%)
  local copies, waits for them, and re-layouts  7.23 us (7%)
  waiting for transfers between devices  6.93 us (7%)
  starting transfers between devices  4.63 us (4%)
    all_gather x1, blocking collectives, shards(): lax.all_gather(local_summ[None, None], 'ctx', axis=1, tiled=True)  43.3 us
    all_gather x1, blocking collectives, shards(): shard_piece = lax.all_gather(per_group, 'grp', axis=0, tiled=True)  13.6 us
    dot_general x1, matrix products, shards(): jnp.einsum('bhqk,bkhd->bhqd', near_weight.astype(jnp.bfloat16), near_vals...  8.5 us
    ppermute x1, waiting for transfers between devices, shifted_2(): return lax.ppermute(value, axis, pairs)  6.93 us
    reduce_sum x1, other arithmetic, shards(): near_total = near_weight.sum(-1)  4.02 us
    dot_general x1, matrix products, update(): jnp.einsum('qhd,rhd->hqr', qheads, tile_keys, preferred_element_type=jnp....  3.38 us
    unnamed x9, local copies, waits for them, and re-layouts  3.26 us
    dot_general x1, matrix products, shards(): jnp.einsum('bqhd,bkhd->bhqk', qheads.reshape(blocks_here, BLK, H, HD), ne...  2.77 us
  transfers between devices with their start and end apart: 2, of which 1 were waited for; matrix products, arithmetic and copies ran while one was open for 6% of the time, Pallas kernels for 0%

commit v1 on v0

v1 whole, which is shorter than its diff:
```python
import functools
import math

import jax
import jax.numpy as jnp
from jax import lax
from jax.experimental import pallas as pl
from jax.experimental.pallas import tpu as pltpu
from jax.sharding import PartitionSpec as P

H = 8
HD = 64
BLK = 512
SUMM = 8
PAIR = 2 * HD
SCALE_LOG2E = math.log2(math.e) / math.sqrt(HD)

masked_score = -1e30
MESH = pl.DeviceIdType.MESH


def at(grp, ctx):
    return (ctx, grp)


def scores_of(q, k):
    return lax.dot_general(q, k, (((1,), (1,)), ((), ())), preferred_element_type=jnp.float32)


def kernel(
    ctx_count, grp_count, pos_ref, q_ref, k_ref, v_ref, out_ref,
    prev_k, prev_v, picked, gathered, sum_k, sum_v, peak_ref, acc_ref,
    near_send, near_recv, ctx_send, ctx_recv, grp_send, grp_recv, own_sem,
):
    me_c = lax.axis_index("ctx")
    me_g = lax.axis_index("grp")
    flat = me_g * ctx_count + me_c
    pairs = H // 2
    early = pairs // 2
    half = BLK // 2
    rows_group = ctx_count * 2 * SUMM
    keys_group = ctx_count * SUMM
    at_last = me_c == ctx_count - 1
    has_next = flat < ctx_count * grp_count - 1
    has_prev = flat > 0

    def ctx_peer(step):
        return lax.rem(me_c + step, ctx_count)

    barrier = pltpu.get_barrier_semaphore()
    for step in range(1, ctx_count):
        pl.semaphore_signal(barrier, inc=1, device_id=at(me_g, ctx_peer(step)), device_id_type=MESH)
    for step in range(1, grp_count):
        @pl.when(me_g >= step)
        def _():
            pl.semaphore_signal(barrier, inc=1, device_id=at(lax.rem(me_g - step + grp_count, grp_count), me_c), device_id_type=MESH)

    @pl.when((me_c == 0) & (me_g > 0))
    def _():
        pl.semaphore_signal(
            barrier, inc=1, device_id=at(lax.rem(me_g - 1 + grp_count, grp_count), ctx_count - 1), device_id_type=MESH
        )

    row = lax.broadcasted_iota(jnp.int32, (2 * SUMM, SUMM), 0)
    slot = lax.broadcasted_iota(jnp.int32, (2 * SUMM, SUMM), 1)
    position = pos_ref[...].astype(jnp.float32)
    target = jnp.where((row & (SUMM - 1)) == slot, position, 0.0).sum(-1, keepdims=True)
    column = lax.broadcasted_iota(jnp.int32, (2 * SUMM, BLK), 1)
    choose = jnp.where(column == target.astype(jnp.int32), 1.0, 0.0).astype(jnp.bfloat16)
    chosen_k = jnp.dot(choose, k_ref[...], preferred_element_type=jnp.float32)
    chosen_v = jnp.dot(choose, v_ref[...], preferred_element_type=jnp.float32)
    wide_row = lax.broadcasted_iota(jnp.int32, chosen_k.shape, 0)
    picked[...] = jnp.where(wide_row < SUMM, chosen_k, chosen_v).astype(jnp.bfloat16)

    wraps = jnp.where(at_last & has_next, 1, 0)
    pl.semaphore_wait(barrier, ctx_count - 1 + grp_count - 1 - me_g + wraps)

    def ctx_copy(step):
        return pltpu.make_async_remote_copy(
            src_ref=picked,
            dst_ref=gathered.at[me_g, me_c],
            send_sem=ctx_send.at[step],
            recv_sem=ctx_recv.at[step],
            device_id=at(me_g, ctx_peer(step)),
            device_id_type=MESH,
        )

    def grp_copy(step):
        return pltpu.make_async_remote_copy(
            src_ref=gathered.at[me_g],
            dst_ref=gathered.at[me_g],
            send_sem=grp_send.at[step],
            recv_sem=grp_recv.at[step],
            device_id=at(lax.rem(me_g + step, grp_count), me_c),
            device_id_type=MESH,
        )

    def near_copy(pair, which):
        columns = pl.ds(pair * PAIR, PAIR)
        source, landing = ((k_ref, prev_k), (v_ref, prev_v))[which]
        wrap = lax.div(me_c + 1, ctx_count)
        return pltpu.make_async_remote_copy(
            src_ref=source.at[:, columns],
            dst_ref=landing.at[:, columns],
            send_sem=near_send.at[2 * pair + which],
            recv_sem=near_recv.at[2 * pair + which],
            device_id=at(lax.rem(me_g + wrap, grp_count), ctx_peer(1)),
            device_id_type=MESH,
        )

    for step in range(1, ctx_count):
        ctx_copy(step).start()

    @pl.when(has_next)
    def _():
        for pair in range(pairs):
            near_copy(pair, 0).start()
            near_copy(pair, 1).start()

    own_copy = pltpu.make_async_copy(
        picked,
        gathered.at[me_g, me_c],
        own_sem,
    )
    own_copy.start()

    lane = lax.broadcasted_iota(jnp.int32, (1, PAIR), 1)
    in_head = [
        jnp.where((lane < HD) == (side == 0), 1.0, 0.0).astype(jnp.bfloat16) for side in range(2)
    ]
    off_head = [in_head[1], in_head[0]]

    def weighed(scores, peak, vals, side):
        weights = jnp.exp2((scores - peak) * SCALE_LOG2E).astype(jnp.bfloat16)
        vals_ones = vals * in_head[side] + off_head[side]
        return jnp.dot(weights, vals_ones, preferred_element_type=jnp.float32)

    def fold(head, side, q, keys, vals, allowed):
        scores = scores_of(q * in_head[side], keys)
        if allowed is not None:
            scores = jnp.where(allowed, scores, masked_score)
        old = peak_ref[head][:, :1]
        peak = jnp.maximum(old, scores.max(-1, keepdims=True))
        part = weighed(scores, peak, vals, side)
        rescale = jnp.exp2((old - peak) * SCALE_LOG2E)
        peak_ref[head] = jnp.broadcast_to(peak, (BLK, PAIR))
        return acc_ref[head] * rescale + part

    def columns_of(pair):
        return pl.ds(pair * PAIR, PAIR)

    def own_pair(pair):
        columns = columns_of(pair)
        for side in range(2):
            head = 2 * pair + side
            for part in range(2):
                rows = pl.ds(part * half, half)
                count = (part + 1) * half
                q = q_ref[rows, columns] * in_head[side]
                scores = scores_of(q, k_ref[pl.ds(0, count), columns])
                u = lax.broadcasted_iota(jnp.int32, scores.shape, 1)
                t = lax.broadcasted_iota(jnp.int32, scores.shape, 0) + part * half
                scores = jnp.where(u <= t, scores, masked_score)
                peak = scores.max(-1, keepdims=True)
                acc_ref[head, rows] = weighed(scores, peak, v_ref[pl.ds(0, count), columns], side)
                peak_ref[head, rows] = jnp.broadcast_to(peak, (half, PAIR))

    for pair in range(early):
        own_pair(pair)

    own_copy.wait()
    for step in range(1, ctx_count):
        ctx_copy(step).wait_recv()
    for step in range(1, grp_count):
        @pl.when(me_g + step < grp_count)
        def _():
            grp_copy(step).start()

    for pair in range(early, pairs):
        own_pair(pair)

    for step in range(1, grp_count):
        @pl.when(me_g >= step)
        def _():
            grp_copy(step).wait_recv()

    key_row = lax.broadcasted_iota(jnp.int32, (keys_group, rows_group), 0)
    source_row = lax.broadcasted_iota(jnp.int32, (keys_group, rows_group), 1)
    wanted = key_row * 2 - (key_row & (SUMM - 1))
    take_k = jnp.where(source_row == wanted, 1.0, 0.0).astype(jnp.bfloat16)
    take_v = jnp.where(source_row == wanted + SUMM, 1.0, 0.0).astype(jnp.bfloat16)
    for group in range(grp_count):
        rows = pl.ds(group * keys_group, keys_group)

        @pl.when(me_g >= group)
        def _():
            block = gathered[group].reshape(rows_group, k_ref.shape[1])
            sum_k[rows] = jnp.dot(take_k, block, preferred_element_type=jnp.float32).astype(
                jnp.bfloat16
            )
            sum_v[rows] = jnp.dot(take_v, block, preferred_element_type=jnp.float32).astype(
                jnp.bfloat16
            )

        @pl.when(me_g < group)
        def _():
            sum_k[rows] = jnp.zeros((keys_group, k_ref.shape[1]), jnp.bfloat16)
            sum_v[rows] = jnp.zeros((keys_group, k_ref.shape[1]), jnp.bfloat16)

    summ_rows = grp_count * keys_group
    tile = math.gcd(summ_rows, BLK)

    def far_pair(pair):
        columns = columns_of(pair)

        def far_tile(index, inner):
            rows = pl.ds(index * tile, tile)
            key_index = lax.broadcasted_iota(jnp.int32, (1, tile), 1) + index * tile
            allowed = key_index < (flat - 1) * SUMM
            for side in range(2):
                head = 2 * pair + side
                acc_ref[head] = fold(
                    head, side, q_ref[:, columns], sum_k[rows, columns], sum_v[rows, columns],
                    allowed,
                )
            return inner

        if summ_rows == tile:
            return far_tile(0, None)
        return lax.fori_loop(0, summ_rows // tile, far_tile, None)

    for pair in range(pairs):
        far_pair(pair)

    def near_pair(pair):
        columns = columns_of(pair)

        @pl.when(has_prev)
        def _():
            near_copy(pair, 0).wait_recv()
            near_copy(pair, 1).wait_recv()
            for side in range(2):
                head = 2 * pair + side
                acc_ref[head] = fold(
                    head, side, q_ref[:, columns], prev_k[:, columns], prev_v[:, columns], None
                )

        even, odd = acc_ref[2 * pair], acc_ref[2 * pair + 1]
        first = lane < HD
        numer = jnp.where(first, even, odd)
        total = pltpu.roll(jnp.where(first, odd, even), HD, 1)
        out_ref[:, columns] = (numer / total).astype(jnp.bfloat16)

    for pair in range(pairs):
        near_pair(pair)

    for step in range(1, ctx_count):
        ctx_copy(step).wait_send()
    for step in range(1, grp_count):
        @pl.when(me_g + step < grp_count)
        def _():
            grp_copy(step).wait_send()

    @pl.when(has_next)
    def _():
        for pair in range(pairs):
            near_copy(pair, 0).wait_send()
            near_copy(pair, 1).wait_send()


def shards(queries, keys, values, summary_pos):
    ctx_count = lax.axis_size("ctx")
    grp_count = lax.axis_size("grp")
    unused, tokens, width = queries.shape
    assert tokens == BLK and width == H * HD
    pairs = H // 2
    group_keys = ctx_count * SUMM
    all_keys = grp_count * group_keys
    vmem = pl.BlockSpec(memory_space=pltpu.VMEM)
    return pl.pallas_call(
        functools.partial(kernel, ctx_count, grp_count),
        out_shape=jax.ShapeDtypeStruct((tokens, width), jnp.bfloat16),
        in_specs=[vmem, vmem, vmem, vmem],
        out_specs=vmem,
        scratch_shapes=[
            pltpu.VMEM((tokens, width), jnp.bfloat16),
            pltpu.VMEM((tokens, width), jnp.bfloat16),
            pltpu.VMEM((2 * SUMM, width), jnp.bfloat16),
            pltpu.VMEM((grp_count, ctx_count, 2 * SUMM, width), jnp.bfloat16),
            pltpu.VMEM((all_keys, width), jnp.bfloat16),
            pltpu.VMEM((all_keys, width), jnp.bfloat16),
            pltpu.VMEM((H, tokens, PAIR), jnp.float32),
            pltpu.VMEM((H, tokens, PAIR), jnp.float32),
            pltpu.SemaphoreType.DMA((2 * pairs,)),
            pltpu.SemaphoreType.DMA((2 * pairs,)),
            pltpu.SemaphoreType.DMA((ctx_count,)),
            pltpu.SemaphoreType.DMA((ctx_count,)),
            pltpu.SemaphoreType.DMA((grp_count,)),
            pltpu.SemaphoreType.DMA((grp_count,)),
            pltpu.SemaphoreType.DMA,
        ],
        compiler_params=pltpu.CompilerParams(
            collective_id=0, has_side_effects=True, vmem_limit_bytes=48 * 1024 * 1024
        ),
    )(summary_pos[0], queries[0], keys[0], values[0])[None]


def solution(mesh):
    placed = (
        P("grp", "ctx", None),
        P("grp", "ctx", None),
        P("grp", "ctx", None),
        P("grp", "ctx", None),
    )
    return jax.shard_map(
        shards, mesh=mesh, in_specs=placed, out_specs=P("grp", "ctx", None), check_vma=False
    )
```

time: 104 us -> 46.9 us (0.45)
  the two profiles are of different devices: /device:TPU:1 before, /device:TPU:2 now
where the time goes in v1:
time: 46.9 us; the launch traced here: 46.6 us
  Pallas kernels  42 us (90%)
  local copies, waits for them, and re-layouts  4.57 us (10%)
    pallas_call x1, Pallas kernels, shards(): pl.pallas_call(functools.partial(kernel, ctx_count, grp_count), out_shape...  42 us
    unnamed x9, local copies, waits for them, and re-layouts  4.57 us

profile of v1, /device:TPU:2, one launch (start us, length us, event | category | flops | bytes accessed | tf_op | source)
XLA Modules:
  0.0 46.6 jit_solution(12074902646271629604)
XLA Ops:
  0.0 0.0 copy-start.3
  0.0 0.7 %copy-done.3 = s32[1,1,8]{2,1,0:T(1,128)S(1)} copy-done((s32[1,1,8]{2,1,0:T(1,128)S(1)}, s32[1,1,8]{2,1,0:T(1,128)}, u32[]{:S(2)}) %copy-start.3) | copy-done | bytes 56
  0.7 0.0 copy-start
  0.7 1.0 %copy-done = bf16[1,512,512]{2,1,0:T(8,128)(2,1)S(1)} copy-done((bf16[1,512,512]{2,1,0:T(8,128)(2,1)S(1)}, bf16[1,512,512]{2,1,0:T(8,128)(2,1)}, u32[]{:S(2)}) %copy-start) | copy-done | bytes 524312
  1.7 0.0 copy-start.1
  1.7 1.0 %copy-done.1 = bf16[1,512,512]{2,1,0:T(8,128)(2,1)S(1)} copy-done((bf16[1,512,512]{2,1,0:T(8,128)(2,1)S(1)}, bf16[1,512,512]{2,1,0:T(8,128)(2,1)}, u32[]{:S(2)}) %copy-start.1) | copy-done | bytes 524312
  2.7 0.0 copy-start.2
  2.7 1.0 %copy-done.2 = bf16[1,512,512]{2,1,0:T(8,128)(2,1)S(1)} copy-done((bf16[1,512,512]{2,1,0:T(8,128)(2,1)S(1)}, bf16[1,512,512]{2,1,0:T(8,128)(2,1)}, u32[]{:S(2)}) %copy-start.2) | copy-done | bytes 524312
  3.8 42.0 %shard_map.46 = bf16[512,512]{1,0:T(8,128)(2,1)S(1)} custom-call(s32[1,8]{1,0:T(1,128)S(1)} %bitcast.9, bf16[512,512]{1,0:T(8,128)(2,1)S(1)} %bitcast.6, bf16[512,512]{1,0:T(8,128)(2,1)S(1)} %bitcast.7, bf16[512,512]{1,0:T(8,128)(2,1)S(1)} %bitcast.8), custom_call_target="tpu_custom_call" | custom-call | tf_op jit(solution)/shard_map/pallas_call | solution.py:280
  45.8 0.8 %copy.6 = bf16[1,512,512]{2,1,0:T(8,128)(2,1)} copy(bf16[1,512,512]{2,1,0:T(8,128)(2,1)S(1)} %bitcast.5) | data formatting | bytes 1048576
Async XLA Ops:
  0.0 0.7 %copy-start.3 = (s32[1,1,8]{2,1,0:T(1,128)S(1)}, s32[1,1,8]{2,1,0:T(1,128)}, u32[]{:S(2)}) copy-start(s32[1,1,8]{2,1,0:T(1,128)} %param.7) | copy-start | bytes 100
  0.7 1.0 %copy-start = (bf16[1,512,512]{2,1,0:T(8,128)(2,1)S(1)}, bf16[1,512,512]{2,1,0:T(8,128)(2,1)}, u32[]{:S(2)}) copy-start(bf16[1,512,512]{2,1,0:T(8,128)(2,1)} %param.4) | copy-start | bytes 1572868
  1.7 1.0 %copy-start.1 = (bf16[1,512,512]{2,1,0:T(8,128)(2,1)S(1)}, bf16[1,512,512]{2,1,0:T(8,128)(2,1)}, u32[]{:S(2)}) copy-start(bf16[1,512,512]{2,1,0:T(8,128)(2,1)} %param.5) | copy-start | bytes 1572868
  2.7 1.0 %copy-start.2 = (bf16[1,512,512]{2,1,0:T(8,128)(2,1)S(1)}, bf16[1,512,512]{2,1,0:T(8,128)(2,1)}, u32[]{:S(2)}) copy-start(bf16[1,512,512]{2,1,0:T(8,128)(2,1)} %param.6) | copy-start | bytes 1572868

commit v2 on v1

--- a/solution.py
+++ b/solution.py
@@ -28,15 +28,16 @@
 
 
 def kernel(
-    ctx_count, grp_count, pos_ref, q_ref, k_ref, v_ref, out_ref,
-    prev_k, prev_v, picked, gathered, sum_k, sum_v, peak_ref, acc_ref,
-    near_send, near_recv, ctx_send, ctx_recv, grp_send, grp_recv, own_sem,
+    ctx_count, grp_count, pos_in, q_in, k_in, v_in, out_ref,
+    pos_ref, q_ref, k_ref, v_ref, prev_k, prev_v, picked, gathered, sum_k, sum_v, peak_ref, acc_ref,
+    near_send, near_recv, ctx_send, ctx_recv, grp_send, grp_recv, own_sem, load_sem,
 ):
     me_c = lax.axis_index("ctx")
     me_g = lax.axis_index("grp")
     flat = me_g * ctx_count + me_c
     pairs = H // 2
-    early = pairs // 2
+    early = 1
+    ahead = 2
     half = BLK // 2
     rows_group = ctx_count * 2 * SUMM
     keys_group = ctx_count * SUMM
@@ -47,6 +48,15 @@
     def ctx_peer(step):
         return lax.rem(me_c + step, ctx_count)
 
+    loads = [
+        pltpu.make_async_copy(source, landing, load_sem.at[number])
+        for number, (source, landing) in enumerate(
+            ((pos_in, pos_ref), (k_in, k_ref), (v_in, v_ref), (q_in, q_ref))
+        )
+    ]
+    for load in loads:
+        load.start()
+
     barrier = pltpu.get_barrier_semaphore()
     for step in range(1, ctx_count):
         pl.semaphore_signal(barrier, inc=1, device_id=at(me_g, ctx_peer(step)), device_id_type=MESH)
@@ -61,6 +71,8 @@
             barrier, inc=1, device_id=at(lax.rem(me_g - 1 + grp_count, grp_count), ctx_count - 1), device_id_type=MESH
         )
 
+    for load in loads[:3]:
+        load.wait()
     row = lax.broadcasted_iota(jnp.int32, (2 * SUMM, SUMM), 0)
     slot = lax.broadcasted_iota(jnp.int32, (2 * SUMM, SUMM), 1)
     position = pos_ref[...].astype(jnp.float32)
@@ -97,7 +109,7 @@
 
     def near_copy(pair, which):
         columns = pl.ds(pair * PAIR, PAIR)
-        source, landing = ((k_ref, prev_k), (v_ref, prev_v))[which]
+        source, landing = ((k_in, prev_k), (v_in, prev_v))[which]
         wrap = lax.div(me_c + 1, ctx_count)
         return pltpu.make_async_remote_copy(
             src_ref=source.at[:, columns],
@@ -111,11 +123,14 @@
     for step in range(1, ctx_count):
         ctx_copy(step).start()
 
-    @pl.when(has_next)
+    def near_start(pair):
+        near_copy(pair, 0).start()
+        near_copy(pair, 1).start()
+
+    @pl.when(has_next & ~at_last)
     def _():
-        for pair in range(pairs):
-            near_copy(pair, 0).start()
-            near_copy(pair, 1).start()
+        for pair in range(ahead):
+            near_start(pair)
 
     own_copy = pltpu.make_async_copy(
         picked,
@@ -123,6 +138,7 @@
         own_sem,
     )
     own_copy.start()
+    loads[3].wait()
 
     lane = lax.broadcasted_iota(jnp.int32, (1, PAIR), 1)
     in_head = [
@@ -171,6 +187,12 @@
     own_copy.wait()
     for step in range(1, ctx_count):
         ctx_copy(step).wait_recv()
+
+    @pl.when(has_next & at_last)
+    def _():
+        for pair in range(ahead):
+            near_start(pair)
+
     for step in range(1, grp_count):
         @pl.when(me_g + step < grp_count)
         def _():
@@ -235,6 +257,13 @@
     def near_pair(pair):
         columns = columns_of(pair)
 
+        @pl.when(has_next)
+        def _():
+            near_copy(pair, 0).wait_send()
+            near_copy(pair, 1).wait_send()
+            if pair + ahead < pairs:
+                near_start(pair + ahead)
+
         @pl.when(has_prev)
         def _():
             near_copy(pair, 0).wait_recv()
@@ -260,12 +289,6 @@
         @pl.when(me_g + step < grp_count)
         def _():
             grp_copy(step).wait_send()
-
-    @pl.when(has_next)
-    def _():
-        for pair in range(pairs):
-            near_copy(pair, 0).wait_send()
-            near_copy(pair, 1).wait_send()
 
 
 def shards(queries, keys, values, summary_pos):
@@ -280,9 +303,13 @@
     return pl.pallas_call(
         functools.partial(kernel, ctx_count, grp_count),
         out_shape=jax.ShapeDtypeStruct((tokens, width), jnp.bfloat16),
-        in_specs=[vmem, vmem, vmem, vmem],
+        in_specs=[pl.BlockSpec(memory_space=pl.ANY)] * 4,
         out_specs=vmem,
         scratch_shapes=[
+            pltpu.VMEM((1, SUMM), jnp.int32),
+            pltpu.VMEM((tokens, width), jnp.bfloat16),
+            pltpu.VMEM((tokens, width), jnp.bfloat16),
+            pltpu.VMEM((tokens, width), jnp.bfloat16),
             pltpu.VMEM((tokens, width), jnp.bfloat16),
             pltpu.VMEM((tokens, width), jnp.bfloat16),
             pltpu.VMEM((2 * SUMM, width), jnp.bfloat16),
@@ -298,9 +325,10 @@
             pltpu.SemaphoreType.DMA((grp_count,)),
             pltpu.SemaphoreType.DMA((grp_count,)),
             pltpu.SemaphoreType.DMA,
+            pltpu.SemaphoreType.DMA((4,)),
         ],
         compiler_params=pltpu.CompilerParams(
-            collective_id=0, has_side_effects=True, vmem_limit_bytes=48 * 1024 * 1024
+            collective_id=0, has_side_effects=True, vmem_limit_bytes=56 * 1024 * 1024
         ),
     )(summary_pos[0], queries[0], keys[0], values[0])[None]
 

time: 46.9 us -> 40.6 us (0.87)
  the two profiles are of different devices: /device:TPU:2 before, /device:TPU:1 now
where the time goes in v2:
time: 40.6 us; the launch traced here: 40.4 us
  Pallas kernels  38.6 us (95%)
  local copies, waits for them, and re-layouts  1.87 us (5%)
    pallas_call x1, Pallas kernels, shards(): pl.pallas_call(functools.partial(kernel, ctx_count, grp_count), out_shape...  38.6 us
    unnamed x1, local copies, waits for them, and re-layouts  1.87 us

profile of v2, /device:TPU:1, one launch (start us, length us, event | category | flops | bytes accessed | tf_op | source)
XLA Modules:
  0.0 40.4 jit_solution(18318952651767648089)
XLA Ops:
  0.0 38.6 %shard_map.46 = bf16[512,512]{1,0:T(8,128)(2,1)} custom-call(s32[1,8]{1,0:T(1,128)} %bitcast.9, bf16[512,512]{1,0:T(8,128)(2,1)} %bitcast.6, bf16[512,512]{1,0:T(8,128)(2,1)} %bitcast.7, bf16[512,512]{1,0:T(8,128)(2,1)} %bitcast.8), custom_call_target="tpu_custom_call" | custom-call | tf_op jit(solution)/shard_map/pallas_call | solution.py:303
  38.6 1.9 %copy.6 = bf16[1,512,512]{2,1,0:T(8,128)(2,1)} copy(bf16[1,512,512]{2,1,0:T(8,128)(2,1)} %bitcast.5) | data formatting | bytes 1048576

commit v3 on v2

--- a/solution.py
+++ b/solution.py
@@ -37,7 +37,7 @@
     flat = me_g * ctx_count + me_c
     pairs = H // 2
     early = 1
-    ahead = 2
+    ahead = pairs - 1
     half = BLK // 2
     rows_group = ctx_count * 2 * SUMM
     keys_group = ctx_count * SUMM
@@ -126,6 +126,10 @@
     def near_start(pair):
         near_copy(pair, 0).start()
         near_copy(pair, 1).start()
+
+    def near_wait_send(pair):
+        near_copy(pair, 0).wait_send()
+        near_copy(pair, 1).wait_send()
 
     @pl.when(has_next & ~at_last)
     def _():
@@ -201,33 +205,34 @@
     for pair in range(early, pairs):
         own_pair(pair)
 
-    for step in range(1, grp_count):
-        @pl.when(me_g >= step)
-        def _():
-            grp_copy(step).wait_recv()
-
     key_row = lax.broadcasted_iota(jnp.int32, (keys_group, rows_group), 0)
     source_row = lax.broadcasted_iota(jnp.int32, (keys_group, rows_group), 1)
     wanted = key_row * 2 - (key_row & (SUMM - 1))
     take_k = jnp.where(source_row == wanted, 1.0, 0.0).astype(jnp.bfloat16)
     take_v = jnp.where(source_row == wanted + SUMM, 1.0, 0.0).astype(jnp.bfloat16)
-    for group in range(grp_count):
-        rows = pl.ds(group * keys_group, keys_group)
-
-        @pl.when(me_g >= group)
-        def _():
-            block = gathered[group].reshape(rows_group, k_ref.shape[1])
-            sum_k[rows] = jnp.dot(take_k, block, preferred_element_type=jnp.float32).astype(
-                jnp.bfloat16
-            )
-            sum_v[rows] = jnp.dot(take_v, block, preferred_element_type=jnp.float32).astype(
-                jnp.bfloat16
-            )
-
-        @pl.when(me_g < group)
-        def _():
-            sum_k[rows] = jnp.zeros((keys_group, k_ref.shape[1]), jnp.bfloat16)
-            sum_v[rows] = jnp.zeros((keys_group, k_ref.shape[1]), jnp.bfloat16)
+    def take_summaries():
+        for step in range(1, grp_count):
+            @pl.when(me_g >= step)
+            def _():
+                grp_copy(step).wait_recv()
+
+        for group in range(grp_count):
+            rows = pl.ds(group * keys_group, keys_group)
+
+            @pl.when(me_g >= group)
+            def _():
+                block = gathered[group].reshape(rows_group, k_ref.shape[1])
+                sum_k[rows] = jnp.dot(take_k, block, preferred_element_type=jnp.float32).astype(
+                    jnp.bfloat16
+                )
+                sum_v[rows] = jnp.dot(take_v, block, preferred_element_type=jnp.float32).astype(
+                    jnp.bfloat16
+                )
+
+            @pl.when(me_g < group)
+            def _():
+                sum_k[rows] = jnp.zeros((keys_group, k_ref.shape[1]), jnp.bfloat16)
+                sum_v[rows] = jnp.zeros((keys_group, k_ref.shape[1]), jnp.bfloat16)
 
     summ_rows = grp_count * keys_group
     tile = math.gcd(summ_rows, BLK)
@@ -251,17 +256,13 @@
             return far_tile(0, None)
         return lax.fori_loop(0, summ_rows // tile, far_tile, None)
 
-    for pair in range(pairs):
-        far_pair(pair)
-
     def near_pair(pair):
         columns = columns_of(pair)
 
-        @pl.when(has_next)
-        def _():
-            near_copy(pair, 0).wait_send()
-            near_copy(pair, 1).wait_send()
-            if pair + ahead < pairs:
+        if pair + ahead < pairs:
+            @pl.when(has_next)
+            def _():
+                near_wait_send(pair)
                 near_start(pair + ahead)
 
         @pl.when(has_prev)
@@ -274,6 +275,8 @@
                     head, side, q_ref[:, columns], prev_k[:, columns], prev_v[:, columns], None
                 )
 
+    def finish_pair(pair):
+        columns = columns_of(pair)
         even, odd = acc_ref[2 * pair], acc_ref[2 * pair + 1]
         first = lane < HD
         numer = jnp.where(first, even, odd)
@@ -281,7 +284,20 @@
         out_ref[:, columns] = (numer / total).astype(jnp.bfloat16)
 
     for pair in range(pairs):
+        if pair == pairs // 2:
+            take_summaries()
+            for far in range(pairs):
+                far_pair(far)
+            for done in range(pair):
+                finish_pair(done)
         near_pair(pair)
+        if pair >= pairs // 2:
+            finish_pair(pair)
+
+    @pl.when(has_next)
+    def _():
+        for pair in range(pairs - ahead, pairs):
+            near_wait_send(pair)
 
     for step in range(1, ctx_count):
         ctx_copy(step).wait_send()

time: 40.6 us -> 40.7 us (level)
  no operation moved by 1% of the time
where the time goes in v3:
time: 40.7 us; the launch traced here: 40.6 us
  Pallas kernels  38.7 us (95%)
  local copies, waits for them, and re-layouts  1.87 us (5%)
    pallas_call x1, Pallas kernels, shards(): pl.pallas_call(functools.partial(kernel, ctx_count, grp_count), out_shape...  38.7 us
    unnamed x1, local copies, waits for them, and re-layouts  1.87 us

profile of v3, /device:TPU:1, one launch (start us, length us, event | category | flops | bytes accessed | tf_op | source)
XLA Modules:
  0.0 40.6 jit_solution(10519640989391053620)
XLA Ops:
  0.0 38.7 %shard_map.46 = bf16[512,512]{1,0:T(8,128)(2,1)} custom-call(s32[1,8]{1,0:T(1,128)} %bitcast.9, bf16[512,512]{1,0:T(8,128)(2,1)} %bitcast.6, bf16[512,512]{1,0:T(8,128)(2,1)} %bitcast.7, bf16[512,512]{1,0:T(8,128)(2,1)} %bitcast.8), custom_call_target="tpu_custom_call" | custom-call | tf_op jit(solution)/shard_map/pallas_call | solution.py:319
  38.7 1.9 %copy.6 = bf16[1,512,512]{2,1,0:T(8,128)(2,1)} copy(bf16[1,512,512]{2,1,0:T(8,128)(2,1)} %bitcast.5) | data formatting | bytes 1048576

commit v4 on v3

--- a/solution.py
+++ b/solution.py
@@ -71,6 +71,54 @@
             barrier, inc=1, device_id=at(lax.rem(me_g - 1 + grp_count, grp_count), ctx_count - 1), device_id_type=MESH
         )
 
+    wraps = jnp.where(at_last & has_next, 1, 0)
+    pl.semaphore_wait(barrier, ctx_count - 1 + grp_count - 1 - me_g + wraps)
+
+    def ctx_copy(step):
+        return pltpu.make_async_remote_copy(
+            src_ref=picked,
+            dst_ref=gathered.at[me_g, me_c],
+            send_sem=ctx_send.at[step],
+            recv_sem=ctx_recv.at[step],
+            device_id=at(me_g, ctx_peer(step)),
+            device_id_type=MESH,
+        )
+
+    def grp_copy(step):
+        return pltpu.make_async_remote_copy(
+            src_ref=gathered.at[me_g],
+            dst_ref=gathered.at[me_g],
+            send_sem=grp_send.at[step],
+            recv_sem=grp_recv.at[step],
+            device_id=at(lax.rem(me_g + step, grp_count), me_c),
+            device_id_type=MESH,
+        )
+
+    def near_copy(pair, which):
+        columns = pl.ds(pair * PAIR, PAIR)
+        source, landing = ((k_in, prev_k), (v_in, prev_v))[which]
+        wrap = lax.div(me_c + 1, ctx_count)
+        return pltpu.make_async_remote_copy(
+            src_ref=source.at[:, columns],
+            dst_ref=landing.at[:, columns],
+            send_sem=near_send.at[2 * pair + which],
+            recv_sem=near_recv.at[2 * pair + which],
+            device_id=at(lax.rem(me_g + wrap, grp_count), ctx_peer(1)),
+            device_id_type=MESH,
+        )
+
+    def near_start(pair):
+        near_copy(pair, 0).start()
+        near_copy(pair, 1).start()
+
+    def near_wait_send(pair):
+        near_copy(pair, 0).wait_send()
+        near_copy(pair, 1).wait_send()
+
+    @pl.when(has_next)
+    def _():
+        near_start(0)
+
     for load in loads[:3]:
         load.wait()
     row = lax.broadcasted_iota(jnp.int32, (2 * SUMM, SUMM), 0)
@@ -84,56 +132,12 @@
     wide_row = lax.broadcasted_iota(jnp.int32, chosen_k.shape, 0)
     picked[...] = jnp.where(wide_row < SUMM, chosen_k, chosen_v).astype(jnp.bfloat16)
 
-    wraps = jnp.where(at_last & has_next, 1, 0)
-    pl.semaphore_wait(barrier, ctx_count - 1 + grp_count - 1 - me_g + wraps)
-
-    def ctx_copy(step):
-        return pltpu.make_async_remote_copy(
-            src_ref=picked,
-            dst_ref=gathered.at[me_g, me_c],
-            send_sem=ctx_send.at[step],
-            recv_sem=ctx_recv.at[step],
-            device_id=at(me_g, ctx_peer(step)),
-            device_id_type=MESH,
-        )
-
-    def grp_copy(step):
-        return pltpu.make_async_remote_copy(
-            src_ref=gathered.at[me_g],
-            dst_ref=gathered.at[me_g],
-            send_sem=grp_send.at[step],
-            recv_sem=grp_recv.at[step],
-            device_id=at(lax.rem(me_g + step, grp_count), me_c),
-            device_id_type=MESH,
-        )
-
-    def near_copy(pair, which):
-        columns = pl.ds(pair * PAIR, PAIR)
-        source, landing = ((k_in, prev_k), (v_in, prev_v))[which]
-        wrap = lax.div(me_c + 1, ctx_count)
-        return pltpu.make_async_remote_copy(
-            src_ref=source.at[:, columns],
-            dst_ref=landing.at[:, columns],
-            send_sem=near_send.at[2 * pair + which],
-            recv_sem=near_recv.at[2 * pair + which],
-            device_id=at(lax.rem(me_g + wrap, grp_count), ctx_peer(1)),
-            device_id_type=MESH,
-        )
-
     for step in range(1, ctx_count):
         ctx_copy(step).start()
 
-    def near_start(pair):
-        near_copy(pair, 0).start()
-        near_copy(pair, 1).start()
-
-    def near_wait_send(pair):
-        near_copy(pair, 0).wait_send()
-        near_copy(pair, 1).wait_send()
-
-    @pl.when(has_next & ~at_last)
+    @pl.when(has_next)
     def _():
-        for pair in range(ahead):
+        for pair in range(1, ahead):
             near_start(pair)
 
     own_copy = pltpu.make_async_copy(
@@ -191,11 +195,6 @@
     own_copy.wait()
     for step in range(1, ctx_count):
         ctx_copy(step).wait_recv()
-
-    @pl.when(has_next & at_last)
-    def _():
-        for pair in range(ahead):
-            near_start(pair)
 
     for step in range(1, grp_count):
         @pl.when(me_g + step < grp_count)

time: 40.7 us -> 42.1 us (1.034)
  the two profiles are of different devices: /device:TPU:1 before, /device:TPU:2 now
where the time goes in v4:
time: 42.1 us; the launch traced here: 41.9 us
  Pallas kernels  40.1 us (95%)
  local copies, waits for them, and re-layouts  1.87 us (4%)
    pallas_call x1, Pallas kernels, shards(): pl.pallas_call(functools.partial(kernel, ctx_count, grp_count), out_shape...  40.1 us
    unnamed x1, local copies, waits for them, and re-layouts  1.87 us

profile of v4, /device:TPU:2, one launch (start us, length us, event | category | flops | bytes accessed | tf_op | source)
XLA Modules:
  0.0 41.9 jit_solution(1540582126078004373)
XLA Ops:
  0.0 40.1 %shard_map.46 = bf16[512,512]{1,0:T(8,128)(2,1)} custom-call(s32[1,8]{1,0:T(1,128)} %bitcast.9, bf16[512,512]{1,0:T(8,128)(2,1)} %bitcast.6, bf16[512,512]{1,0:T(8,128)(2,1)} %bitcast.7, bf16[512,512]{1,0:T(8,128)(2,1)} %bitcast.8), custom_call_target="tpu_custom_call" | custom-call | tf_op jit(solution)/shard_map/pallas_call | solution.py:318
  40.1 1.9 %copy.6 = bf16[1,512,512]{2,1,0:T(8,128)(2,1)} copy(bf16[1,512,512]{2,1,0:T(8,128)(2,1)} %bitcast.5) | data formatting | bytes 1048576

commit v5 on v4

--- a/solution.py
+++ b/solution.py
@@ -31,13 +31,16 @@
     ctx_count, grp_count, pos_in, q_in, k_in, v_in, out_ref,
     pos_ref, q_ref, k_ref, v_ref, prev_k, prev_v, picked, gathered, sum_k, sum_v, peak_ref, acc_ref,
     near_send, near_recv, ctx_send, ctx_recv, grp_send, grp_recv, own_sem, load_sem,
+    relay, relay_send, relay_recv, onward_send,
 ):
     me_c = lax.axis_index("ctx")
     me_g = lax.axis_index("grp")
     flat = me_g * ctx_count + me_c
     pairs = H // 2
     early = 1
-    ahead = pairs - 1
+    relayed = pairs // 2
+    first_ctx = me_c == 0
+    relays = first_ctx & (me_g < grp_count - 1)
     half = BLK // 2
     rows_group = ctx_count * 2 * SUMM
     keys_group = ctx_count * SUMM
@@ -107,13 +110,49 @@
             device_id_type=MESH,
         )
 
+    def relay_copy(pair, which):
+        slot = 2 * (pair - relayed) + which
+        return pltpu.make_async_remote_copy(
+            src_ref=(k_in, v_in)[which].at[:, pl.ds(pair * PAIR, PAIR)],
+            dst_ref=relay.at[slot],
+            send_sem=relay_send.at[slot],
+            recv_sem=relay_recv.at[slot],
+            device_id=at(me_g, ctx_peer(1)),
+            device_id_type=MESH,
+        )
+
+    def onward_copy(pair, which):
+        slot = 2 * (pair - relayed) + which
+        return pltpu.make_async_remote_copy(
+            src_ref=relay.at[slot],
+            dst_ref=(prev_k, prev_v)[which].at[:, pl.ds(pair * PAIR, PAIR)],
+            send_sem=onward_send.at[slot],
+            recv_sem=near_recv.at[2 * pair + which],
+            device_id=at(lax.rem(me_g + 1, grp_count), me_c),
+            device_id_type=MESH,
+        )
+
+    def near_each(pair, act):
+        if pair < relayed:
+            for which in range(2):
+                act(near_copy(pair, which))
+            return
+
+        @pl.when(at_last)
+        def _():
+            for which in range(2):
+                act(relay_copy(pair, which))
+
+        @pl.when(~at_last)
+        def _():
+            for which in range(2):
+                act(near_copy(pair, which))
+
     def near_start(pair):
-        near_copy(pair, 0).start()
-        near_copy(pair, 1).start()
+        near_each(pair, lambda copy: copy.start())
 
     def near_wait_send(pair):
-        near_copy(pair, 0).wait_send()
-        near_copy(pair, 1).wait_send()
+        near_each(pair, lambda copy: copy.wait_send())
 
     @pl.when(has_next)
     def _():
@@ -137,7 +176,7 @@
 
     @pl.when(has_next)
     def _():
-        for pair in range(1, ahead):
+        for pair in range(1, pairs):
             near_start(pair)
 
     own_copy = pltpu.make_async_copy(
@@ -258,12 +297,6 @@
     def near_pair(pair):
         columns = columns_of(pair)
 
-        if pair + ahead < pairs:
-            @pl.when(has_next)
-            def _():
-                near_wait_send(pair)
-                near_start(pair + ahead)
-
         @pl.when(has_prev)
         def _():
             near_copy(pair, 0).wait_recv()
@@ -281,6 +314,13 @@
         numer = jnp.where(first, even, odd)
         total = pltpu.roll(jnp.where(first, odd, even), HD, 1)
         out_ref[:, columns] = (numer / total).astype(jnp.bfloat16)
+
+    @pl.when(relays)
+    def _():
+        for pair in range(relayed, pairs):
+            for which in range(2):
+                relay_copy(pair, which).wait_recv()
+                onward_copy(pair, which).start()
 
     for pair in range(pairs):
         if pair == pairs // 2:
@@ -295,8 +335,14 @@
 
     @pl.when(has_next)
     def _():
-        for pair in range(pairs - ahead, pairs):
+        for pair in range(pairs):
             near_wait_send(pair)
+
+    @pl.when(relays)
+    def _():
+        for pair in range(relayed, pairs):
+            for which in range(2):
+                onward_copy(pair, which).wait_send()
 
     for step in range(1, ctx_count):
         ctx_copy(step).wait_send()
@@ -341,6 +387,10 @@
             pltpu.SemaphoreType.DMA((grp_count,)),
             pltpu.SemaphoreType.DMA,
             pltpu.SemaphoreType.DMA((4,)),
+            pltpu.VMEM((pairs, tokens, PAIR), jnp.bfloat16),
+            pltpu.SemaphoreType.DMA((pairs,)),
+            pltpu.SemaphoreType.DMA((pairs,)),
+            pltpu.SemaphoreType.DMA((pairs,)),
         ],
         compiler_params=pltpu.CompilerParams(
             collective_id=0, has_side_effects=True, vmem_limit_bytes=56 * 1024 * 1024

time: 42.1 us -> 47.5 us (1.13)
  the two profiles are of different devices: /device:TPU:2 before, /device:TPU:1 now
where the time goes in v5:
time: 47.5 us; the launch traced here: 47.3 us
  Pallas kernels  45.4 us (96%)
  local copies, waits for them, and re-layouts  1.87 us (4%)
    pallas_call x1, Pallas kernels, shards(): pl.pallas_call(functools.partial(kernel, ctx_count, grp_count), out_shape...  45.4 us
    unnamed x1, local copies, waits for them, and re-layouts  1.87 us

profile of v5, /device:TPU:1, one launch (start us, length us, event | category | flops | bytes accessed | tf_op | source)
XLA Modules:
  0.0 47.3 jit_solution(2619734509255828791)
XLA Ops:
  0.0 45.4 %shard_map.46 = bf16[512,512]{1,0:T(8,128)(2,1)} custom-call(s32[1,8]{1,0:T(1,128)} %bitcast.9, bf16[512,512]{1,0:T(8,128)(2,1)} %bitcast.6, bf16[512,512]{1,0:T(8,128)(2,1)} %bitcast.7, bf16[512,512]{1,0:T(8,128)(2,1)} %bitcast.8), custom_call_target="tpu_custom_call" | custom-call | tf_op jit(solution)/shard_map/pallas_call | solution.py:364
  45.4 1.9 %copy.6 = bf16[1,512,512]{2,1,0:T(8,128)(2,1)} copy(bf16[1,512,512]{2,1,0:T(8,128)(2,1)} %bitcast.5) | data formatting | bytes 1048576

commit v6 on v4

--- a/solution.py
+++ b/solution.py
@@ -37,7 +37,7 @@
     flat = me_g * ctx_count + me_c
     pairs = H // 2
     early = 1
-    ahead = pairs - 1
+    ahead = pairs
     half = BLK // 2
     rows_group = ctx_count * 2 * SUMM
     keys_group = ctx_count * SUMM

time: 42.1 us -> 47.5 us (1.13)
  Pallas kernels: 40.1 us -> 45.5 us
    pallas_call x1, Pallas kernels: 40.1 us -> 45.5 us  [shards(): pl.pallas_call(functools.partial(kernel, ctx_count, grp_count), out_shape...]
where the time goes in v6:
time: 47.5 us; the launch traced here: 47.4 us
  Pallas kernels  45.5 us (96%)
  local copies, waits for them, and re-layouts  1.87 us (4%)
    pallas_call x1, Pallas kernels, shards(): pl.pallas_call(functools.partial(kernel, ctx_count, grp_count), out_shape...  45.5 us
    unnamed x1, local copies, waits for them, and re-layouts  1.87 us

profile of v6, /device:TPU:2, one launch (start us, length us, event | category | flops | bytes accessed | tf_op | source)
XLA Modules:
  0.0 47.4 jit_solution(5911433529335510887)
XLA Ops:
  0.0 45.5 %shard_map.46 = bf16[512,512]{1,0:T(8,128)(2,1)} custom-call(s32[1,8]{1,0:T(1,128)} %bitcast.9, bf16[512,512]{1,0:T(8,128)(2,1)} %bitcast.6, bf16[512,512]{1,0:T(8,128)(2,1)} %bitcast.7, bf16[512,512]{1,0:T(8,128)(2,1)} %bitcast.8), custom_call_target="tpu_custom_call" | custom-call | tf_op jit(solution)/shard_map/pallas_call | solution.py:318
  45.5 1.9 %copy.6 = bf16[1,512,512]{2,1,0:T(8,128)(2,1)} copy(bf16[1,512,512]{2,1,0:T(8,128)(2,1)} %bitcast.5) | data formatting | bytes 1048576
